TPU v7x, 256 devices: a whole 4x4x8 slice. The times are simulated.
256 devices in a mesh: blk: 16 (over y, z_lo, core), win: 16 (over x, z_hi).
Axes of the slice: x: 4, y: 4, z: 8 (z_hi: 4, z_lo: 2; z = z_hi * 2 + z_lo), core: 2. Of those that a mesh axis runs over, the one named last changes fastest.
Arguments:
- spectra: float32 [2, 64, 192, 4096], P(None, 'win', None, 'blk'), may hold values from -6 to 6
- masks: int32 [64, 4096], P('win', 'blk'), may hold values 0 or 1
- plan: int32 [2, 16], replicated, may hold values from 0 to 15, as said below
Outputs:
- correlations: float32 [2, 4096, 32, 256], P(None, ('blk', 'win'))
Inputs may be any that keep to these rules, and one draw needn't show every extreme that they name: `plan`: in round r every block b has partner b XOR m_r for one nonzero m_r of that round; the m_r differ between rounds.
All inputs are finite; a program needn't handle non-finite values. No bound on the sum of `masks` on one device may be relied on, other than what follows from the above.
Results may differ from a plain program's by a relative error of at most 0.0003.
Values sent between devices are 32-bit elements; how exact they have to be, the bound alone decides.
No kernel may reach another device: no remote copies, remote signals or barrier semaphores. Data moves between devices by JAX's collectives and lax.ppermute only.
A program may use at most 128 MiB of HBM per device.

v0:
```python
import math

import jax
import jax.numpy as jnp
from jax import lax
from jax.sharding import PartitionSpec as P

LAGS = 32


def from_partner(block, axis, apart):
    count = lax.axis_size(axis)
    route = []
    for low in range(count):
        high = low | 1 << apart
        if high != low and high < count:
            route += [(low, high), (high, low)]
    return lax.ppermute(block, axis, route)


def fetch_partner(held, offset, bit_list):
    for bit in bit_list:
        other = from_partner(held, "blk", bit)
        held = jnp.where(offset >> bit & 1 == 1, other, held)
    return held


def on_device(spectra, masks, plan):
    high = lax.Precision.HIGHEST
    power = jnp.mean(spectra[0] * spectra[0] + spectra[1] * spectra[1], axis=1, keepdims=True)
    scale = masks[:, None, :].astype(jnp.float32) * lax.rsqrt(power + 1e-06)
    white = spectra * scale[None]
    local = lax.all_to_all(white, "win", split_axis=2, concat_axis=1, tiled=True)
    groups = lax.axis_size("win")
    share = local.shape[2]
    bins = share * groups
    windows = local.shape[1]
    norm = 1.0 / math.sqrt(windows * bins)
    blocks_count = lax.axis_size("blk")
    nbits = blocks_count.bit_length() - 1
    bit_list = list(range(nbits))
    shift = (jnp.arange(LAGS) - LAGS // 2).astype(jnp.float32)
    outputs = []
    for r in range(plan.shape[0]):
        offset = plan[r, 0]
        partner = fetch_partner(local, offset, bit_list)
        real = jnp.einsum("wfi,wfj->fij", local[0], partner[0], precision=high) + jnp.einsum(
            "wfi,wfj->fij", local[1], partner[1], precision=high
        )
        imag = jnp.einsum("wfi,wfj->fij", local[0], partner[1], precision=high) - jnp.einsum(
            "wfi,wfj->fij", local[1], partner[0], precision=high
        )
        first = lax.axis_index("win") * share
        freq = (first + jnp.arange(share)).astype(jnp.float32)
        angle = math.pi * shift[:, None] * freq[None, :] / bins
        cos_t = jnp.cos(angle)
        sin_t = jnp.sin(angle)
        lagged = jnp.einsum("lf,fij->ilj", cos_t, real, precision=high) - jnp.einsum(
            "lf,fij->ilj", sin_t, imag, precision=high
        )
        result = lax.psum_scatter(lagged * norm, "win", scatter_dimension=0, tiled=True)
        outputs.append(result)
    return jnp.stack(outputs, axis=0)


def solution(mesh):
    return jax.shard_map(
        on_device,
        mesh=mesh,
        in_specs=(P(None, "win", None, "blk"), P("win", "blk"), P()),
        out_specs=P(None, ("blk", "win"), None, None),
        check_vma=False,
    )
```

profile of v0, /device:TPU:1, one launch (start us, length us, event | category | flops | bytes accessed | tf_op | source)
XLA Modules:
  0.0 527.2 jit_solution(9133462912955282187)
XLA Ops:
  6.5 1.5 add_reduce_fusion
  8.0 0.7 rsqrt_multiply_fusion
  8.7 2.4 copy_multiply_fusion
  11.2 49.7 %all_to_all.18 = f32[2,4,192,256]{3,1,0,2:T(4,128)S(1)} all-to-all(f32[2,4,192,256]{3,1,0,2:T(4,128)S(1)} %copy_multiply_fusion), channel_id=1, replica_groups=mesh['blk'=16,'win'=16] {'win'}, dimensions={2} | all-to-all | bytes 3145728 | tf_op jit(solution)/shard_map/all_to_all | solution.py:33
  60.9 0.8 copy.23
  61.7 4.3 collective-permute-start
  66.1 0.5 fusion.61
  67.9 1.2 collective-permute-done
  69.1 2.4 broadcast_select_fusion.4
  72.1 35.0 %collective-permute-done.4 = f32[2,64,12,256]{3,0,2,1:T(2,128)S(1)} collective-permute-done((f32[2,64,12,256]{3,0,2,1:T(2,128)S(1)}, f32[2,64,12,256]{3,0,2,1:T(2,128)S(1)}, u32[]{:S(2)}, u32[]{:S(2)}) %collective-permute-start.4) | collective-permute-done | bytes 1572896 | tf_op jit(solution)/shard_map/ppermute | solution.py:18
  107.1 0.2 broadcast_select_fusion.1
  107.3 1.4 collective-permute-start.5
  109.3 32.7 %collective-permute-done.5 = f32[2,64,12,256]{3,0,2,1:T(2,128)S(1)} collective-permute-done((f32[2,64,12,256]{3,0,2,1:T(2,128)S(1)}, f32[2,64,12,256]{3,0,2,1:T(2,128)S(1)}, u32[]{:S(2)}, u32[]{:S(2)}) %collective-permute-start.5) | collective-permute-done | bytes 1572896 | tf_op jit(solution)/shard_map/ppermute | solution.py:18
  142.1 0.2 broadcast_select_fusion.2
  142.3 3.2 collective-permute-start.6
  146.1 0.3 copy.21
  146.4 1.2 fusion.60
  147.7 0.3 squeeze.14
  148.0 2.2 copy.22
  150.2 1.4 squeeze.12
  151.6 26.3 %collective-permute-done.6 = f32[2,64,12,256]{3,0,2,1:T(2,128)} collective-permute-done((f32[2,64,12,256]{3,0,2,1:T(2,128)S(1)}, f32[2,64,12,256]{3,0,2,1:T(2,128)}, u32[]{:S(2)}, u32[]{:S(2)}) %collective-permute-start.6) | collective-permute-done | bytes 1572896 | tf_op jit(solution)/shard_map/ppermute | solution.py:18
  177.9 1.6 broadcast_select_fusion.3
  179.5 1.2 fusion.59
  180.7 2.8 fusion.15
  183.5 2.8 fusion.13
  186.3 2.9 convolution_subtract_fusion
  189.2 3.3 convolution_add_fusion
  192.5 9.2 %fusion = f32[256,256,32]{1,2,0:T(8,128)S(1)} fusion(f32[12,256,256]{2,1,0:T(8,128)S(1)} %convolution_subtract_fusion, f32[12]{0:T(128)S(1)} %add_convert_fusion, f32[32]{0:T(128)S(1)} %convert_multiply_fusion), kind=kOutput, calls=%fused_computation.2 | convolution fusion | flops 301990656 | bytes 11534512 | tf_op jit(solution)/shard_map/lf,fij->ilj/dot_general | solution.py:58
  201.7 11.8 %multiply_bitcast_fusion = f32[256,32,256]{2,1,0:T(8,128)} fusion(f32[256,256,32]{1,2,0:T(8,128)S(1)} %fusion, f32[12,256,256]{2,1,0:T(8,128)S(1)} %convolution_add_fusion, f32[12]{0:T(128)S(1)} %add_convert_fusion, f32[32]{0:T(128)S(1)} %convert_multiply_fusion), kind=kOutput, calls=%fused_computation | convolution fusion | flops 306184960 | bytes 19923120 | tf_op jit(solution)/shard_map/lf,fij->ilj/dot_general | solution.py:58
  213.5 1.3 copy-done
  214.9 1.0 collective-permute-start.1
  216.5 77.2 %collective-permute-done.1 = f32[2,64,12,256]{3,0,2,1:T(2,128)S(1)} collective-permute-done((f32[2,64,12,256]{3,0,2,1:T(2,128)S(1)}, f32[2,64,12,256]{3,0,2,1:T(2,128)S(1)}, u32[]{:S(2)}, u32[]{:S(2)}) %collective-permute-start.1) | collective-permute-done | bytes 1572896 | tf_op jit(solution)/shard_map/ppermute | solution.py:18
  293.6 0.2 broadcast_select_fusion.5
  293.9 1.2 collective-permute-start.2
  295.6 18.0 %collective-permute-done.2 = f32[2,64,12,256]{3,0,2,1:T(2,128)S(1)} collective-permute-done((f32[2,64,12,256]{3,0,2,1:T(2,128)S(1)}, f32[2,64,12,256]{3,0,2,1:T(2,128)S(1)}, u32[]{:S(2)}, u32[]{:S(2)}) %collective-permute-start.2) | collective-permute-done | bytes 1572896 | tf_op jit(solution)/shard_map/ppermute | solution.py:18
  313.6 0.2 broadcast_select_fusion.6
  313.8 3.4 collective-permute-start.3
  317.8 32.9 %collective-permute-done.3 = f32[2,64,12,256]{3,0,2,1:T(2,128)S(1)} collective-permute-done((f32[2,64,12,256]{3,0,2,1:T(2,128)S(1)}, f32[2,64,12,256]{3,0,2,1:T(2,128)S(1)}, u32[]{:S(2)}, u32[]{:S(2)}) %collective-permute-start.3) | collective-permute-done | bytes 1572896 | tf_op jit(solution)/shard_map/ppermute | solution.py:18
  350.7 0.2 broadcast_select_fusion.7
  350.9 1.2 fusion.58
  352.1 2.8 fusion.21
  354.9 2.8 fusion.19
  357.6 2.9 convolution_subtract_fusion.1
  360.6 3.1 convolution_add_fusion.1
  363.7 9.2 %fusion.4 = f32[256,256,32]{1,2,0:T(8,128)S(1)} fusion(f32[12,256,256]{2,1,0:T(8,128)S(1)} %convolution_subtract_fusion.1, f32[12]{0:T(128)S(1)} %add_convert_fusion, f32[32]{0:T(128)S(1)} %convert_multiply_fusion), kind=kOutput, calls=%fused_computation.6 | convolution fusion | flops 301990656 | bytes 11534512 | tf_op jit(solution)/shard_map/lf,fij->ilj/dot_general | solution.py:58
  372.9 12.0 %multiply_bitcast_fusion.1 = f32[256,32,256]{2,1,0:T(8,128)} fusion(f32[256,256,32]{1,2,0:T(8,128)S(1)} %fusion.4, f32[12,256,256]{2,1,0:T(8,128)S(1)} %convolution_add_fusion.1, f32[12]{0:T(128)S(1)} %add_convert_fusion, f32[32]{0:T(128)S(1)} %convert_multiply_fusion), kind=kOutput, calls=%fused_computation.1 | convolution fusion | flops 306184960 | bytes 19923120 | tf_op jit(solution)/shard_map/lf,fij->ilj/dot_general | solution.py:58
  384.9 132.9 %reduce-scatter.3.cloned.1.call-done = f32[16,32,256]{2,1,0:T(8,128)} async-done(((f32[256,32,256]{2,1,0:T(8,128)}), f32[16,32,256]{2,1,0:T(8,128)}) %reduce-scatter.3.cloned.1.call-update) | async-done | bytes 524304 | tf_op jit(solution)/shard_map/reduce_scatter | solution.py:61
  517.9 2.3 pad_maximum_fusion
  (12 shorter events, 0.3 us)
Async XLA Ops:
  6.5 378.4 %reduce-scatter.5.cloned.1.call-start = ((), (), s32[]{:S(2)}) async-start(), calls=%async_computation.4 | async-start | bytes 8912896 | tf_op jit(solution)/shard_map/reduce_scatter | solution.py:61
  11.2 54.9 %copy-start.1 = (s32[2,16]{1,0:T(2,128)S(1)}, s32[2,16]{1,0:T(2,128)}, u32[]{:S(2)}) copy-start(s32[2,16]{1,0:T(2,128)} %param.5) | copy-start | bytes 388
  61.7 7.4 %collective-permute-start = (f32[2,64,12,256]{3,0,2,1:T(2,128)S(1)}, f32[2,64,12,256]{3,0,2,1:T(2,128)S(1)}, u32[]{:S(2)}, u32[]{:S(2)}) collective-permute-start(f32[2,64,12,256]{3,0,2,1:T(2,128)S(1)} %bitcast.91), channel_id=1, source_target_pairs={{0,16},{16,0},{32,48},{48,32},{64,80},{80,64},{96,112},{112,96},{1... | collective-permute-start | bytes 4718600 | tf_op jit(solution)/shard_map/ppermute | solution.py:18
  71.5 35.6 %collective-permute-start.4 = (f32[2,64,12,256]{3,0,2,1:T(2,128)S(1)}, f32[2,64,12,256]{3,0,2,1:T(2,128)S(1)}, u32[]{:S(2)}, u32[]{:S(2)}) collective-permute-start(f32[2,64,12,256]{3,0,2,1:T(2,128)S(1)} %get-tuple-element.6), channel_id=1, source_target_pairs={{0,32},{32,0},{16,48},{48,16},{64,96},{96,64},{80,112},{112,80},{1... | collective-permute-start | bytes 4718600 | tf_op jit(solution)/shard_map/ppermute | solution.py:18
  107.3 34.8 %collective-permute-start.5 = (f32[2,64,12,256]{3,0,2,1:T(2,128)S(1)}, f32[2,64,12,256]{3,0,2,1:T(2,128)S(1)}, u32[]{:S(2)}, u32[]{:S(2)}) collective-permute-start(f32[2,64,12,256]{3,0,2,1:T(2,128)S(1)} %bitcast.85), channel_id=1, source_target_pairs={{0,64},{64,0},{16,80},{80,16},{32,96},{96,32},{48,112},{112,48},{1... | collective-permute-start | bytes 4718600 | tf_op jit(solution)/shard_map/ppermute | solution.py:18
  142.3 35.6 %collective-permute-start.6 = (f32[2,64,12,256]{3,0,2,1:T(2,128)S(1)}, f32[2,64,12,256]{3,0,2,1:T(2,128)}, u32[]{:S(2)}, u32[]{:S(2)}) collective-permute-start(f32[2,64,12,256]{3,0,2,1:T(2,128)S(1)} %bitcast.82), channel_id=1, source_target_pairs={{0,128},{128,0},{16,144},{144,16},{32,160},{160,32},{48,176},{176,... | collective-permute-start | bytes 4718600 | tf_op jit(solution)/shard_map/ppermute | solution.py:18
  213.5 1.4 copy-start
  213.5 304.4 %reduce-scatter.3.cloned.1.call-start = ((), (), s32[]{:S(2)}) async-start(), calls=%async_computation.3 | async-start | bytes 8912896 | tf_op jit(solution)/shard_map/reduce_scatter | solution.py:61
  214.9 78.8 %collective-permute-start.1 = (f32[2,64,12,256]{3,0,2,1:T(2,128)S(1)}, f32[2,64,12,256]{3,0,2,1:T(2,128)S(1)}, u32[]{:S(2)}, u32[]{:S(2)}) collective-permute-start(f32[2,64,12,256]{3,0,2,1:T(2,128)S(1)} %copy-done), channel_id=1, source_target_pairs={{0,32},{32,0},{16,48},{48,16},{64,96},{96,64},{80,112},{112,80},{1... | collective-permute-start | bytes 4718600 | tf_op jit(solution)/shard_map/ppermute | solution.py:18
  293.9 19.8 %collective-permute-start.2 = (f32[2,64,12,256]{3,0,2,1:T(2,128)S(1)}, f32[2,64,12,256]{3,0,2,1:T(2,128)S(1)}, u32[]{:S(2)}, u32[]{:S(2)}) collective-permute-start(f32[2,64,12,256]{3,0,2,1:T(2,128)S(1)} %bitcast.84), channel_id=1, source_target_pairs={{0,64},{64,0},{16,80},{80,16},{32,96},{96,32},{48,112},{112,48},{1... | collective-permute-start | bytes 4718600 | tf_op jit(solution)/shard_map/ppermute | solution.py:18
  313.8 36.9 %collective-permute-start.3 = (f32[2,64,12,256]{3,0,2,1:T(2,128)S(1)}, f32[2,64,12,256]{3,0,2,1:T(2,128)S(1)}, u32[]{:S(2)}, u32[]{:S(2)}) collective-permute-start(f32[2,64,12,256]{3,0,2,1:T(2,128)S(1)} %bitcast.83), channel_id=1, source_target_pairs={{0,128},{128,0},{16,144},{144,16},{32,160},{160,32},{48,176},{176,... | collective-permute-start | bytes 4718600 | tf_op jit(solution)/shard_map/ppermute | solution.py:18
Sparse Core Ops, SparseCore 0:
  213.6 137.6 reduce-scatter.4
  385.0 132.7 reduce-scatter.2
where the time goes:
time: 533 us; the launch traced here: 527 us
  waiting for transfers between devices  356 us (67%)
  matrix products  65.4 us (12%)
  blocking collectives  49.7 us (9%)
  between operations  18.9 us (4%)
  starting transfers between devices  14.5 us (3%)
  other arithmetic  11.9 us (2%)
  local copies, waits for them, and re-layouts  10.6 us (2%)
    ppermute x7, waiting for transfers between devices, from_partner(): return lax.ppermute(block, axis, route)  223 us
    reduce_scatter x2, waiting for transfers between devices, on_device(): lax.psum_scatter(lagged * norm, 'win', scatter_dimension=0, tiled=True)  133 us
    all_to_all x1, blocking collectives, on_device(): lax.all_to_all(white, 'win', split_axis=2, concat_axis=1, tiled=True)  49.7 us
    dot_general x2, matrix products, on_device(): jnp.einsum('lf,fij->ilj', cos_t, real, precision=high)  23.8 us
    dot_general x2, matrix products, on_device(): jnp.einsum('lf,fij->ilj', sin_t, imag, precision=high)  18.3 us
    ppermute x7, starting transfers between devices, from_partner(): return lax.ppermute(block, axis, route)  14.5 us
  transfers between devices with their start and end apart: 9, of which 8 were waited for; matrix products, arithmetic and copies ran while one was open for 8% of the time, Pallas kernels for 0%

commit v1 on v0

v1 whole, which is shorter than its diff:
```python
import functools
import math

import jax
import jax.numpy as jnp
import ml_dtypes
import numpy as np
from jax import lax
from jax.experimental import pallas as pl
from jax.experimental.pallas import tpu as pltpu
from jax.sharding import Mesh
from jax.sharding import PartitionSpec as P

LAGS = 32
BINS = 192
WINDOWS = 64
HALF = BINS // 2
STEP = 16
STEPS = HALF // STEP


def lag_table():
    tau = np.arange(LAGS) - LAGS // 2
    norm = 1.0 / math.sqrt(WINDOWS * BINS)
    bins = np.arange(BINS).reshape(2, STEPS, STEP).transpose(1, 2, 0)
    theta = np.pi * bins[..., None] * tau / BINS
    both = np.stack([np.cos(theta), -np.sin(theta)], axis=3) * norm
    table = np.einsum("sfhpl,jk->sjlfhpk", both, np.eye(8))
    table = table.reshape(STEPS, 8 * LAGS, STEP * 4 * 8).astype(np.float32)
    high = table.astype(ml_dtypes.bfloat16)
    low = (table - high.astype(np.float32)).astype(ml_dtypes.bfloat16)
    return high, low


def halves(value):
    high = value.astype(jnp.bfloat16)
    return high, (value - high.astype(jnp.float32)).astype(jnp.bfloat16)


def whiten_kernel(spectra_ref, masks_ref, own_ref, rows_ref):
    parts, windows, bins, channels = spectra_ref.shape
    pieces = []
    scales = []
    for w in range(windows):
        a, b = spectra_ref[0, w], spectra_ref[1, w]
        power = jnp.sum(a * a + b * b, axis=0, keepdims=True) * (1.0 / bins)
        scales.append(masks_ref[w : w + 1, :].astype(jnp.float32) * lax.rsqrt(power + 1e-06))
    for p in range(parts):
        for w in range(windows):
            pieces.append(spectra_ref[p, w] * scales[w])
    white = jnp.swapaxes(jnp.stack(pieces, axis=0), 0, 1)
    own_ref[...] = white
    lane = lax.broadcasted_iota(jnp.int32, (HALF, 8, 128), 2)
    for block in range(channels // 128):
        a = white[:HALF, :, block * 128 : (block + 1) * 128]
        b = white[HALF:, :, block * 128 : (block + 1) * 128]
        rows_ref[2 * block] = jnp.where(lane < 64, a, pltpu.roll(b, 64, axis=2))
        rows_ref[2 * block + 1] = jnp.where(lane < 64, pltpu.roll(a, 64, axis=2), b)


def whiten(spectra, masks):
    return pl.pallas_call(
        whiten_kernel,
        out_shape=(
            jax.ShapeDtypeStruct((BINS, 8, 256), jnp.float32),
            jax.ShapeDtypeStruct((4, HALF, 8, 128), jnp.float32),
        ),
        compiler_params=pltpu.CompilerParams(vmem_limit_bytes=32 * 2**20),
        name="whiten",
    )(spectra, masks)


def stack_kernel(rows_ref, own_ref, high_ref, low_ref, out_ref, prod_ref):
    step = pl.program_id(0)
    sign = jnp.where(lax.broadcasted_iota(jnp.int32, (4, 8, 128), 1) < 4, -1.0, 1.0)

    def one_low(f, _):
        p = rows_ref[:, f]
        q = pltpu.roll(p, 4, axis=1) * sign
        left = jnp.concatenate([p.reshape(32, 128), q.reshape(32, 128)], axis=1)
        lh, ll = halves(left)
        left = jnp.concatenate([lh, lh, ll], axis=0).T
        for h in range(2):
            right = own_ref[:, h, f].reshape(32, 256)
            rh, rl = halves(right)
            right = jnp.concatenate([rh, rl, rh], axis=0)
            rows = jnp.concatenate([left[64 * h : 64 * h + 64], left[128 + 64 * h : 192 + 64 * h]], axis=0)
            prod_ref[2 * f + h] = jnp.dot(rows, right, preferred_element_type=jnp.float32).reshape(2, 64, 256)
        return 0

    lax.fori_loop(0, STEP, one_low, 0, unroll=4)

    @pl.when(step == 0)
    def _():
        out_ref[...] = jnp.zeros_like(out_ref)

    gh, gl = high_ref[0], low_ref[0]
    for t in range(8):
        value = prod_ref[:, :, 8 * t : 8 * t + 8].reshape(STEP * 32, 256)
        vh, vl = halves(value)
        dot = functools.partial(jnp.dot, preferred_element_type=jnp.float32)
        lagged = dot(gh, vh) + dot(gl, vh) + dot(gh, vl)
        out_ref[8 * t : 8 * t + 8] += lagged.reshape(8, LAGS, 256)


def stack(rows, own, high, low):
    own = own.reshape(4, 2, HALF, 8, 256)
    return pl.pallas_call(
        stack_kernel,
        grid=(STEPS,),
        in_specs=[
            pl.BlockSpec((4, STEP, 8, 128), lambda s: (0, s, 0, 0)),
            pl.BlockSpec((4, 2, STEP, 8, 256), lambda s: (0, 0, s, 0, 0)),
            pl.BlockSpec((1, 8 * LAGS, STEP * 32), lambda s: (s, 0, 0)),
            pl.BlockSpec((1, 8 * LAGS, STEP * 32), lambda s: (s, 0, 0)),
        ],
        out_specs=pl.BlockSpec((64, LAGS, 256), lambda s: (0, 0, 0)),
        out_shape=jax.ShapeDtypeStruct((64, LAGS, 256), jnp.float32),
        scratch_shapes=[pltpu.VMEM((2 * STEP, 2, 64, 256), jnp.float32)],
        compiler_params=pltpu.CompilerParams(vmem_limit_bytes=40 * 2**20),
        cost_estimate=pl.CostEstimate(flops=16 * 10**9, bytes_accessed=14 * 2**20, transcendentals=0),
        name="stack",
    )(rows, own, high, low)


def to_partner(value, offset):
    count = lax.axis_size("blk")

    def by(mask):
        return lambda v: lax.ppermute(v, "blk", [(b, b ^ mask) for b in range(count)])

    return lax.switch(offset - 1, [by(mask) for mask in range(1, count)], value)


def on_device(spectra, masks, plan):
    high, low = (jnp.asarray(t) for t in lag_table())
    own, rows = whiten(spectra, masks)
    own = lax.all_gather(own, "x", axis=0, tiled=False)
    rows = lax.all_to_all(rows, "x", split_axis=0, concat_axis=0, tiled=True)
    rounds = plan.shape[0]
    theirs = [to_partner(rows, plan[r, 0]) for r in range(rounds)]
    partial = [stack(theirs[r], own, high, low) for r in range(rounds)]
    sums = [lax.psum_scatter(partial[r], "zh", scatter_dimension=0, tiled=True) for r in range(rounds)]
    return jnp.stack([to_partner(sums[r], plan[r, 0]) for r in range(rounds)], axis=0)


def solution(mesh):
    fine = Mesh(mesh.devices.reshape(16, 4, 4), ("blk", "x", "zh"))
    return jax.shard_map(
        on_device,
        mesh=fine,
        in_specs=(P(None, ("x", "zh"), None, "blk"), P(("x", "zh"), "blk"), P()),
        out_specs=P(None, ("blk", "x", "zh"), None, None),
        check_vma=False,
    )
```

time: 533 us -> 289 us (0.54)
  waiting for transfers between devices: 356 us -> 196 us
  matrix products: 65.4 us -> 0 us
  blocking collectives: 49.7 us -> 0 us
  Pallas kernels: 0 us -> 45.6 us
  other arithmetic: 11.9 us -> 2.28 us
  starting transfers between devices: 14.5 us -> 20.1 us
    ppermute x7 -> x4, waiting for transfers between devices: 223 us -> 123 us  [by(): lax.ppermute(v, 'blk', [(b, b ^ mask) for b in range(count)])]
    reduce_scatter x2, waiting for transfers between devices: 133 us -> 40.7 us  [on_device(): lax.psum_scatter(partial[r], 'zh', scatter_dimension=0, tiled=True)]
    dot_general x12 -> x0, matrix products: 65.4 us -> none  [the longest x2 23.8 us: on_device(): jnp.einsum('lf,fij->ilj', cos_t, real, precision=high)]
    all_to_all x1 -> x0, blocking collectives: 49.7 us -> none  [on_device(): lax.all_to_all(white, 'win', split_axis=2, concat_axis=1, tiled=True)]
    pallas_call x0 -> x3, Pallas kernels: none -> 45.6 us  [the longest x2 43.5 us: stack(): pl.pallas_call(stack_kernel, grid=(STEPS,), in_specs=[pl.BlockSpec((4, ST...]
    all_to_all x0 -> x1, waiting for transfers between devices: none -> 18.6 us  [on_device(): rows = lax.all_to_all(rows, 'x', split_axis=0, concat_axis=0, tiled=True)]
    all_gather x0 -> x1, waiting for transfers between devices: none -> 13.1 us  [on_device(): own = lax.all_gather(own, 'x', axis=0, tiled=False)]
    unnamed x4 -> x14, local copies, waits for them, and re-layouts: 1.34 us -> 7.67 us
  transfers between devices with their start and end apart: 9 -> 8, of which waited for: 8 -> 7; matrix products, arithmetic and copies ran while one was open for 8% -> 0% of each run, Pallas kernels for 0% -> 8%
where the time goes in v1:
time: 289 us; the launch traced here: 287 us
  waiting for transfers between devices  196 us (68%)
  Pallas kernels  45.6 us (16%)
  starting transfers between devices  20.1 us (7%)
  between operations  14.7 us (5%)
  local copies, waits for them, and re-layouts  8.25 us (3%)
    ppermute x4, waiting for transfers between devices, by(): lax.ppermute(v, 'blk', [(b, b ^ mask) for b in range(count)])  123 us
    pallas_call x2, Pallas kernels, stack(): pl.pallas_call(stack_kernel, grid=(STEPS,), in_specs=[pl.BlockSpec((4, ST...  43.5 us
    reduce_scatter x2, waiting for transfers between devices, on_device(): lax.psum_scatter(partial[r], 'zh', scatter_dimension=0, tiled=True)  40.7 us
    all_to_all x1, waiting for transfers between devices, on_device(): rows = lax.all_to_all(rows, 'x', split_axis=0, concat_axis=0, tiled=True)  18.6 us
    ppermute x4, starting transfers between devices, by(): lax.ppermute(v, 'blk', [(b, b ^ mask) for b in range(count)])  14.9 us
    all_gather x1, waiting for transfers between devices, on_device(): own = lax.all_gather(own, 'x', axis=0, tiled=False)  13.1 us
    unnamed x14, local copies, waits for them, and re-layouts  7.67 us
  transfers between devices with their start and end apart: 8, of which 7 were waited for; matrix products, arithmetic and copies ran while one was open for 0% of the time, Pallas kernels for 8%

profile of v1, /device:TPU:1, one launch (start us, length us, event | category | flops | bytes accessed | tf_op | source)
XLA Modules:
  0.0 287.4 jit_solution(6824765066921966932)
XLA Ops:
  6.5 0.0 all-gather.3.cloned.1.call-start
  6.5 0.0 copy-start
  6.5 1.4 copy-done
  7.9 0.0 copy-start.1
  7.9 0.7 copy-done.1
  8.6 2.1 whiten.1
  10.8 0.0 copy-start.6
  10.8 0.0 all-gather.3.cloned.1.call-update
  10.8 0.0 copy-start.4
  10.8 0.0 copy-start.5
  10.8 5.1 %all-to-all-start = ((f32[4,96,8,128]{3,2,1,0:T(8,128)}), f32[4,96,8,128]{3,2,1,0:T(8,128)}, u32[]{:S(2)}, u32[]{:S(2)}) async-start(f32[4,96,8,128]{3,2,1,0:T(8,128)} %get-tuple-element.133), calls=%async_computation | async-start | bytes 3145728 | tf_op jit(solution)/shard_map/all_to_all | solution.py:139
  15.9 0.0 reduce-scatter.3.cloned.1.call-start
  16.0 0.0 copy-done.6
  16.0 0.6 fusion
  17.2 18.6 %all-to-all-done = f32[4,96,8,128]{3,2,1,0:T(8,128)} async-done(((f32[4,96,8,128]{3,2,1,0:T(8,128)}), f32[4,96,8,128]{3,2,1,0:T(8,128)}, u32[]{:S(2)}, u32[]{:S(2)}) %all-to-all-start) | async-done | bytes 1572896 | tf_op jit(solution)/shard_map/all_to_all | solution.py:139
  35.8 39.4 %conditional.4 = (f32[4,96,8,128]{3,2,1,0:T(8,128)}) conditional(s32[]{:T(128)} %bitcast.30, f32[4,96,8,128]{3,2,1,0:T(8,128)} %all-to-all-done, f32[4,96,8,128]{3,2,1,0:T(8,128)} %all-to-all-done, f32[4,96,8,128]{3,2,1,0:T(8,128)} %all-to-all-done, f32[4,96,8,128]{3,2,1,0:T(8,128)} %all-to-all-done, ...), branch_computations={%region_0.0_spmd, %region_1.0_spmd, %region_2.0_spmd, %region_3.0_... | conditional | bytes 6291504 | solution.py:132
  35.8 9.1 %collective-permute-start.9 = (f32[4,96,8,128]{3,2,1,0:T(8,128)}, f32[4,96,8,128]{3,2,1,0:T(8,128)}, u32[]{:S(2)}, u32[]{:S(2)}) collective-permute-start(f32[4,96,8,128]{3,2,1,0:T(8,128)} %param.9), channel_id=1, source_target_pairs={{0,160},{16,176},{32,128},{48,144},{64,224},{80,240},{96,192},{112... | collective-permute-start | bytes 4718600 | tf_op jit(solution)/shard_map/cond/branch_9_fun/ppermute | solution.py:130
  44.9 30.2 %collective-permute-done.9 = f32[4,96,8,128]{3,2,1,0:T(8,128)} collective-permute-done((f32[4,96,8,128]{3,2,1,0:T(8,128)}, f32[4,96,8,128]{3,2,1,0:T(8,128)}, u32[]{:S(2)}, u32[]{:S(2)}) %collective-permute-start.9) | collective-permute-done | bytes 1572896 | tf_op jit(solution)/shard_map/cond/branch_9_fun/ppermute | solution.py:130
  75.2 13.1 %all-gather.3.cloned.1.call-done = f32[768,8,256]{2,1,0:T(8,128)} async-done(((f32[192,8,256]{2,1,0:T(8,128)}), f32[768,8,256]{2,1,0:T(8,128)}) %all-gather.3.cloned.1.call-update) | async-done | bytes 6291472 | tf_op jit(solution)/shard_map/all_gather | solution.py:138
  88.2 0.0 copy-done.4
  88.2 0.0 copy-done.5
  88.2 0.0 copy-start.2
  88.2 2.8 copy-done.2
  91.0 21.8 %stack.98 = f32[64,32,256]{2,1,0:T(8,128)} custom-call(f32[4,96,8,128]{3,2,1,0:T(8,128)} %get-tuple-element.137.rows_ref, f32[4,2,96,8,256]{4,3,2,1,0:T(8,128)S(1)} %bitcast.33, bf16[6,256,512]{2,1,0:T(8,128)(2,1)S(1)} %copy-done.4, bf16[6,256,512]{2,1,0:T(8,128)(2,1)S(1)} %copy-done.5), custom_call_target="tpu_custom_call" | custom-call | flops 16000000000 | bytes 14680064 | tf_op jit(solution)/shard_map/stack/pallas_call | solution.py:108
  112.8 0.0 reduce-scatter.3.cloned.1.call-update
  112.8 0.0 reduce-scatter.5.cloned.1.call-start
  113.6 70.7 %conditional.6 = (f32[4,96,8,128]{3,2,1,0:T(8,128)}) conditional(s32[]{:T(128)} %bitcast.32, f32[4,96,8,128]{3,2,1,0:T(8,128)} %all-to-all-done, f32[4,96,8,128]{3,2,1,0:T(8,128)} %all-to-all-done, f32[4,96,8,128]{3,2,1,0:T(8,128)} %all-to-all-done, f32[4,96,8,128]{3,2,1,0:T(8,128)} %all-to-all-done, ...), branch_computations={%region_31.0_spmd, %region_32.0_spmd, %region_33.0_spmd, %region_3... | conditional | bytes 6291504 | solution.py:132
  113.6 1.9 collective-permute-start.31
  115.5 68.4 %collective-permute-done.31 = f32[4,96,8,128]{3,2,1,0:T(8,128)} collective-permute-done((f32[4,96,8,128]{3,2,1,0:T(8,128)}, f32[4,96,8,128]{3,2,1,0:T(8,128)}, u32[]{:S(2)}, u32[]{:S(2)}) %collective-permute-start.31) | collective-permute-done | bytes 1572896 | tf_op jit(solution)/shard_map/cond/branch_1_fun/ppermute | solution.py:130
  184.2 0.0 copy-start.3
  184.2 2.8 copy-done.3
  187.0 21.7 %stack.99 = f32[64,32,256]{2,1,0:T(8,128)} custom-call(f32[4,96,8,128]{3,2,1,0:T(8,128)} %get-tuple-element.139.rows_ref, f32[4,2,96,8,256]{4,3,2,1,0:T(8,128)S(1)} %bitcast.34, bf16[6,256,512]{2,1,0:T(8,128)(2,1)S(1)} %copy-done.4, bf16[6,256,512]{2,1,0:T(8,128)(2,1)S(1)} %copy-done.5), custom_call_target="tpu_custom_call" | custom-call | flops 16000000000 | bytes 14680064 | tf_op jit(solution)/shard_map/stack/pallas_call | solution.py:108
  208.7 0.0 reduce-scatter.5.cloned.1.call-update
  208.7 0.0 reduce-scatter.3.cloned.1.call-done
  208.8 15.5 %conditional.5 = (f32[1,16,32,256]{3,2,1,0:T(8,128)}) conditional(s32[]{:T(128)} %bitcast.30, f32[16,32,256]{2,1,0:T(8,128)} %reduce-scatter.3.cloned.1.call-done, f32[16,32,256]{2,1,0:T(8,128)} %reduce-scatter.3.cloned.1.call-done, f32[16,32,256]{2,1,0:T(8,128)} %reduce-scatter.3.cloned.1.call-done, ...), branch_computations={%region_16.0_spmd, %region_17.0_spmd, %region_18.0_spmd, %region_1... | conditional | bytes 2097200 | solution.py:132
  208.8 3.9 %collective-permute-start.24 = (f32[16,32,256]{2,1,0:T(8,128)}, f32[16,32,256]{2,1,0:T(8,128)}, u32[]{:S(2)}, u32[]{:S(2)}) collective-permute-start(f32[16,32,256]{2,1,0:T(8,128)} %param.24), channel_id=1, source_target_pairs={{0,160},{16,176},{32,128},{48,144},{64,224},{80,240},{96,192},{112... | collective-permute-start | bytes 1572872 | tf_op jit(solution)/shard_map/cond/branch_9_fun/ppermute | solution.py:130
  212.7 11.5 %collective-permute-done.24 = f32[16,32,256]{2,1,0:T(8,128)} collective-permute-done((f32[16,32,256]{2,1,0:T(8,128)}, f32[16,32,256]{2,1,0:T(8,128)}, u32[]{:S(2)}, u32[]{:S(2)}) %collective-permute-start.24) | collective-permute-done | bytes 524320 | tf_op jit(solution)/shard_map/cond/branch_9_fun/ppermute | solution.py:130
  224.3 40.7 %reduce-scatter.5.cloned.1.call-done = f32[16,32,256]{2,1,0:T(8,128)} async-done(((f32[64,32,256]{2,1,0:T(8,128)}), f32[16,32,256]{2,1,0:T(8,128)}) %reduce-scatter.5.cloned.1.call-update) | async-done | bytes 524304 | tf_op jit(solution)/shard_map/reduce_scatter | solution.py:143
  265.0 13.4 %conditional.7 = (f32[1,16,32,256]{3,2,1,0:T(8,128)}) conditional(s32[]{:T(128)} %bitcast.32, f32[16,32,256]{2,1,0:T(8,128)} %reduce-scatter.5.cloned.1.call-done, f32[16,32,256]{2,1,0:T(8,128)} %reduce-scatter.5.cloned.1.call-done, f32[16,32,256]{2,1,0:T(8,128)} %reduce-scatter.5.cloned.1.call-done, ...), branch_computations={%region_47.0_spmd, %region_48.0_spmd, %region_49.0_spmd, %region_5... | conditional | bytes 2097200 | solution.py:132
  265.0 0.0 collective-permute-start.46
  265.0 13.4 %collective-permute-done.46 = f32[16,32,256]{2,1,0:T(8,128)} collective-permute-done((f32[16,32,256]{2,1,0:T(8,128)}, f32[16,32,256]{2,1,0:T(8,128)}, u32[]{:S(2)}, u32[]{:S(2)}) %collective-permute-start.46) | collective-permute-done | bytes 524320 | tf_op jit(solution)/shard_map/cond/branch_1_fun/ppermute | solution.py:130
  278.4 2.3 pad_maximum_fusion
Async XLA Ops:
  6.5 81.7 %all-gather.3.cloned.1.call-start = ((), (), s32[]{:S(2)}) async-start(), calls=%async_computation.5 | async-start | bytes 7864320 | tf_op jit(solution)/shard_map/all_gather | solution.py:138
  6.5 1.4 copy-start
  7.9 0.7 copy-start.1
  10.8 5.2 %copy-start.6 = (s32[2,16]{1,0:T(2,128)S(1)}, s32[2,16]{1,0:T(2,128)}, u32[]{:S(2)}) copy-start(s32[2,16]{1,0:T(2,128)} %param.67) | copy-start | bytes 388
  10.8 77.4 %copy-start.4 = (bf16[6,256,512]{2,1,0:T(8,128)(2,1)S(1)}, bf16[6,256,512]{2,1,0:T(8,128)(2,1)}, u32[]{:S(2)}) copy-start(bf16[6,256,512]{2,1,0:T(8,128)(2,1)} %constant.18.clone.high_ref) | copy-start | bytes 4718596
  10.8 77.4 %copy-start.5 = (bf16[6,256,512]{2,1,0:T(8,128)(2,1)S(1)}, bf16[6,256,512]{2,1,0:T(8,128)(2,1)}, u32[]{:S(2)}) copy-start(bf16[6,256,512]{2,1,0:T(8,128)(2,1)} %constant.19.clone.low_ref) | copy-start | bytes 4718596
  10.8 25.0 %all-to-all-start = ((f32[4,96,8,128]{3,2,1,0:T(8,128)}), f32[4,96,8,128]{3,2,1,0:T(8,128)}, u32[]{:S(2)}, u32[]{:S(2)}) async-start(f32[4,96,8,128]{3,2,1,0:T(8,128)} %get-tuple-element.133), calls=%async_computation | async-start | bytes 3145728 | tf_op jit(solution)/shard_map/all_to_all | solution.py:139
  15.9 192.8 %reduce-scatter.3.cloned.1.call-start = ((), (), s32[]{:S(2)}) async-start(), calls=%async_computation.3 | async-start | bytes 2621440 | tf_op jit(solution)/shard_map/reduce_scatter | solution.py:143
  35.8 39.4 %collective-permute-start.9 = (f32[4,96,8,128]{3,2,1,0:T(8,128)}, f32[4,96,8,128]{3,2,1,0:T(8,128)}, u32[]{:S(2)}, u32[]{:S(2)}) collective-permute-start(f32[4,96,8,128]{3,2,1,0:T(8,128)} %param.9), channel_id=1, source_target_pairs={{0,160},{16,176},{32,128},{48,144},{64,224},{80,240},{96,192},{112... | collective-permute-start | bytes 4718600 | tf_op jit(solution)/shard_map/cond/branch_9_fun/ppermute | solution.py:130
  88.2 2.8 copy-start.2
  112.8 152.2 %reduce-scatter.5.cloned.1.call-start = ((), (), s32[]{:S(2)}) async-start(), calls=%async_computation.4 | async-start | bytes 2621440 | tf_op jit(solution)/shard_map/reduce_scatter | solution.py:143
  113.6 70.3 %collective-permute-start.31 = (f32[4,96,8,128]{3,2,1,0:T(8,128)}, f32[4,96,8,128]{3,2,1,0:T(8,128)}, u32[]{:S(2)}, u32[]{:S(2)}) collective-permute-start(f32[4,96,8,128]{3,2,1,0:T(8,128)} %param.31), channel_id=1, source_target_pairs={{0,32},{16,48},{32,0},{48,16},{64,96},{80,112},{96,64},{112,80},{1... | collective-permute-start | bytes 4718600 | tf_op jit(solution)/shard_map/cond/branch_1_fun/ppermute | solution.py:130
  184.2 2.8 copy-start.3
  208.8 15.3 %collective-permute-start.24 = (f32[16,32,256]{2,1,0:T(8,128)}, f32[16,32,256]{2,1,0:T(8,128)}, u32[]{:S(2)}, u32[]{:S(2)}) collective-permute-start(f32[16,32,256]{2,1,0:T(8,128)} %param.24), channel_id=1, source_target_pairs={{0,160},{16,176},{32,128},{48,144},{64,224},{80,240},{96,192},{112... | collective-permute-start | bytes 1572872 | tf_op jit(solution)/shard_map/cond/branch_9_fun/ppermute | solution.py:130
  265.0 13.4 %collective-permute-start.46 = (f32[16,32,256]{2,1,0:T(8,128)}, f32[16,32,256]{2,1,0:T(8,128)}, u32[]{:S(2)}, u32[]{:S(2)}) collective-permute-start(f32[16,32,256]{2,1,0:T(8,128)} %param.46), channel_id=1, source_target_pairs={{0,32},{16,48},{32,0},{48,16},{64,96},{80,112},{96,64},{112,80},{1... | collective-permute-start | bytes 1572872 | tf_op jit(solution)/shard_map/cond/branch_1_fun/ppermute | solution.py:130
Sparse Core Ops, SparseCore 0:
  10.9 77.2 all-gather.2
  113.0 68.7 reduce-scatter.2
  208.9 56.0 reduce-scatter.4
